TPU v7x, 32 devices: a whole 2x2x4 slice. The times are simulated.
32 devices in a mesh: wide: 8 (over z, x), narrow: 4 (over y, core).
Axes of the slice: x: 2, y: 2, z: 4, core: 2. Of those that a mesh axis runs over, the one named last changes fastest.
Arguments:
- trial_x: float32 [65536, 128], P(('wide', 'narrow')), may hold values from -6 to 6
- trial_y: float32 [65536, 128], P(('wide', 'narrow')), may hold values from -6 to 6
- energy: float32 [65536], P(('wide', 'narrow')), may hold values from 1 to 4
- level_shift: float32 [128], replicated, may hold values from 0.1 to 0.5
- resonant_kernel: bfloat16 [256, 8, 256, 256], P(('wide', 'narrow')), may hold values from -0.0625 to 0.0625
- resonant_list: int32 [256, 8], P(('wide', 'narrow')), may hold values from 0 to 31, all different within a row
- coupling_kernel: bfloat16 [256, 8, 256, 256], P(('wide', 'narrow')), may hold values from -0.0625 to 0.0625
- coupling_list: int32 [256, 8], P(('wide', 'narrow')), may hold values from 0 to 31, all different within a row
- partner: int32 [8, 8192], P('wide'), may hold values from 0 to 8191, each once within a row
- exchange_basis: bfloat16 [65536, 1024], P(('wide', 'narrow')), may hold values from -0.046875 to 0.046875
Outputs:
- new_x: float32 [65536, 128], P(('wide', 'narrow'))
- new_y: float32 [65536, 128], P(('wide', 'narrow'))
Inputs may be any that keep to these rules, and one draw needn't show every extreme that they name: `resonant_list`: each row lists 8 different column blocks. `coupling_list`: each row lists 8 different column blocks. `partner`: each row is a permutation of the patch rows.
All inputs are finite; a program needn't handle non-finite values.
Results may differ from a plain program's by a relative error of at most 0.0038.
Values may be sent and summed in bfloat16 or wider, within the bound.
A program may use at most 128 MiB of HBM per device.

v0:
```python
import jax
import jax.numpy as jnp
from jax import lax
from jax.sharding import PartitionSpec as P

BLK = 256
APPS = 2


def swapped(array, axis, stride):
    return lax.ppermute(array, axis, [(i, i ^ 1 << stride) for i in range(lax.axis_size(axis))])


def block_product(kernel, source, indices):
    columns = source.shape[1]
    tiles = source[indices]
    result = jnp.einsum("bnij,bnjc->bic", kernel, tiles, preferred_element_type=jnp.float32)
    return result.reshape(-1, columns)


def mirror_rows(stacked):
    top_bit = lax.axis_size("wide").bit_length() - 2
    moved = swapped(stacked, "wide", top_bit)
    return lax.all_gather(moved, "narrow", axis=0, tiled=True)


def exchange_term(summed, exchange_basis):
    basis_cols = exchange_basis
    share = lax.psum_scatter(
        lax.dot_general(
            basis_cols, summed, (((0,), (0,)), ((), ())), preferred_element_type=jnp.float32
        ),
        "narrow",
        scatter_dimension=0,
        tiled=True,
    )
    share = lax.psum(share, "wide")
    basis_cols = exchange_basis
    return jnp.dot(
        basis_cols,
        lax.all_gather(share.astype(jnp.bfloat16), "narrow", axis=0, tiled=True),
        preferred_element_type=jnp.float32,
    )


def apply_once(
    trial_x,
    trial_y,
    energy,
    level_shift,
    resonant_kernel,
    resonant_list,
    coupling_kernel,
    coupling_list,
    partner,
    exchange_basis,
):
    vectors = trial_x.shape[1]
    stacked = jnp.concatenate([trial_x.astype(jnp.bfloat16), trial_y.astype(jnp.bfloat16)], axis=1)
    own_patch = lax.all_gather(stacked, "narrow", axis=0, tiled=True)
    mirror_patch = mirror_rows(stacked)
    offsets = jnp.arange(BLK, dtype=jnp.int32)
    own_indices = resonant_list[:, :, None] * BLK + offsets
    resonant = block_product(resonant_kernel, own_patch, own_indices)
    partner_indices = partner[0].reshape(-1, BLK)[coupling_list]
    coupling = block_product(coupling_kernel, mirror_patch, partner_indices)
    summed = (trial_x + trial_y).astype(jnp.bfloat16)
    exchange = exchange_term(summed, exchange_basis)
    levels = energy[:, None]
    shifts = level_shift[None, :]
    image_x = levels * trial_x + resonant[:, :vectors] + coupling[:, vectors:] + exchange
    image_y = -(levels * trial_y + resonant[:, vectors:] + coupling[:, :vectors] + exchange)
    next_x = (image_x - shifts * trial_x) / (levels - shifts)
    next_y = -(image_y - shifts * trial_y) / (levels + shifts)
    return (next_x, next_y)


def on_device(
    trial_x,
    trial_y,
    energy,
    level_shift,
    resonant_kernel,
    resonant_list,
    coupling_kernel,
    coupling_list,
    partner,
    exchange_basis,
):
    current_x, current_y = (trial_x, trial_y)
    for app_index in range(APPS):
        current_x, current_y = apply_once(
            current_x,
            current_y,
            energy,
            level_shift,
            resonant_kernel,
            resonant_list,
            coupling_kernel,
            coupling_list,
            partner,
            exchange_basis,
        )
    return (current_x, current_y)


def solution(mesh):
    return jax.shard_map(
        on_device,
        mesh=mesh,
        in_specs=(
            P(("wide", "narrow"), None),
            P(("wide", "narrow"), None),
            P(("wide", "narrow")),
            P(),
            P(("wide", "narrow"), None, None, None),
            P(("wide", "narrow"), None),
            P(("wide", "narrow"), None, None, None),
            P(("wide", "narrow"), None),
            P("wide", None),
            P(("wide", "narrow"), None),
        ),
        out_specs=(P(("wide", "narrow"), None), P(("wide", "narrow"), None)),
        check_vma=False,
    )
```

profile of v0, /device:TPU:0, one launch (start us, length us, event | category | flops | bytes accessed | tf_op | source)
XLA Modules:
  0.0 539.4 jit_solution(2911928501564749800)
XLA Ops:
  7.3 4.5 convolution_bitcast_fusion.3
  14.4 4.1 collective-permute-start
  18.5 45.8 %collective-permute-done = bf16[2048,256]{1,0:T(8,128)(2,1)S(1)} collective-permute-done((bf16[2048,256]{1,0:T(8,128)(2,1)}, bf16[2048,256]{1,0:T(8,128)(2,1)S(1)}, u32[]{:S(2)}, u32[]{:S(2)}) %collective-permute-start) | collective-permute-done | bytes 1048608 | tf_op jit(solution)/shard_map/ppermute | solution.py:11
  69.4 39.1 %all-reduce.2 = bf16[256,128]{0,1:T(8,128)(2,1)S(1)} all-reduce(f32[256,128]{0,1:T(8,128)} %reduce-scatter.3.cloned.1.call-done), channel_id=1, replica_groups=mesh['wide'=8,'narrow'=4] {'wide'}, use_global_device_ids=true, to_apply=%region_1.0 | all-reduce | flops 32768 | bytes 196608 | tf_op jit(solution)/shard_map/psum | solution.py:37
  108.5 5.8 %all_gather.20 = bf16[1024,128]{0,1:T(8,128)(2,1)S(1)} all-gather(bf16[256,128]{0,1:T(8,128)(2,1)S(1)} %all-reduce.2), channel_id=1, replica_groups=mesh['wide'=8,'narrow'=4] {'narrow'}, dimensions={0}, use_global_device_ids=true | all-gather | bytes 327680 | tf_op jit(solution)/shard_map/all_gather | solution.py:41
  114.3 63.5 %gather_fusion = bf16[16384,256]{1,0:T(8,128)(2,1)} fusion(bf16[8192,256]{1,0:T(8,128)(2,1)} %all-gather.5.cloned.1.call-done, s32[16384]{0:T(1024)S(1)} %broadcast_clamp_fusion.1), kind=kCustom, calls=%fused_computation | custom fusion | bytes 16842752 | tf_op jit(solution)/shard_map/gather | solution.py:16
  177.9 8.1 %fusion.8 = f32[8,256,256,1]{1,2,3,0:T(8,128)S(1)} fusion(bf16[8,8,256,256]{3,2,1,0:T(8,128)(2,1)} %param.14, bf16[8,8,256,256]{3,2,1,0:T(8,128)(2,1)} %bitcast.62), kind=kOutput, calls=%fused_computation.32 | convolution fusion | flops 2147483648 | bytes 18874368 | tf_op jit(solution)/shard_map/bnij,bnjc->bic/dot_general | solution.py:17
  186.1 1.4 copy.32
  188.8 63.5 %gather_fusion.2 = bf16[16384,256]{1,0:T(8,128)(2,1)} fusion(bf16[8192,256]{1,0:T(8,128)(2,1)} %all-gather.7.cloned.1.call-done, s32[16384]{0:T(1024)S(1)} %broadcast_clamp_fusion), kind=kCustom, calls=%fused_computation.2 | custom fusion | bytes 16842752 | tf_op jit(solution)/shard_map/gather | solution.py:16
  252.3 8.1 %fusion.9 = f32[8,256,256,1]{1,2,3,0:T(8,128)S(1)} fusion(bf16[8,8,256,256]{3,2,1,0:T(8,128)(2,1)} %param.16, bf16[8,8,256,256]{3,2,1,0:T(8,128)(2,1)} %bitcast.63), kind=kOutput, calls=%fused_computation.33 | convolution fusion | flops 2147483648 | bytes 18874368 | tf_op jit(solution)/shard_map/bnij,bnjc->bic/dot_general | solution.py:17
  260.6 1.3 copy.33
  262.3 5.5 %fusion.3 = (bf16[2048,128]{0,1:T(8,128)(2,1)S(1)}, f32[2048,128]{0,1:T(8,128)S(1)}, bf16[2048,128]{0,1:T(8,128)(2,1)S(1)}, f32[2048,128]{0,1:T(8,128)S(1)}) fusion(f32[2048,128]{0,1:T(8,128)} %copy.16, f32[128]{0:T(128)S(1)} %copy-done.11, f32[2048,128]{0,1:T(8,128)S(1)} %copy.35, f32[2048,128]{0,1:T(8,128)} %copy.34, f32[2048]{0:T(1024)S(1)} %copy-done.10, ...), kind=kOutput, calls=%fused_computation.27 | convolution fusion | flops 542113792 | bytes 13902336 | tf_op jit(solution)/shard_map/dot_general | solution.py:39
  269.1 1.5 convolution_bitcast_fusion.2
  271.9 47.2 %collective-permute-done.1 = bf16[2048,256]{0,1:T(8,128)(2,1)S(1)} collective-permute-done((bf16[2048,256]{0,1:T(8,128)(2,1)}, bf16[2048,256]{0,1:T(8,128)(2,1)S(1)}, u32[]{:S(2)}, u32[]{:S(2)}) %collective-permute-start.1) | collective-permute-done | bytes 1048608 | tf_op jit(solution)/shard_map/ppermute | solution.py:11
  320.1 36.5 %all-reduce.3 = bf16[256,128]{0,1:T(8,128)(2,1)S(1)} all-reduce(f32[256,128]{0,1:T(8,128)} %reduce-scatter.5.cloned.1.call-done), channel_id=1, replica_groups=mesh['wide'=8,'narrow'=4] {'wide'}, use_global_device_ids=true, to_apply=%region_3.0 | all-reduce | flops 32768 | bytes 196608 | tf_op jit(solution)/shard_map/psum | solution.py:37
  356.6 6.3 %all_gather.23 = bf16[1024,128]{0,1:T(8,128)(2,1)S(1)} all-gather(bf16[256,128]{0,1:T(8,128)(2,1)S(1)} %all-reduce.3), channel_id=1, replica_groups=mesh['wide'=8,'narrow'=4] {'narrow'}, dimensions={0}, use_global_device_ids=true | all-gather | bytes 327680 | tf_op jit(solution)/shard_map/all_gather | solution.py:41
  362.9 6.4 %copy.20 = bf16[8192,256]{1,0:T(8,128)(2,1)} copy(bf16[8192,256]{0,1:T(8,128)(2,1)} %all-gather.9.cloned.1.call-done) | data formatting | bytes 8388608 | tf_op jit(solution)/shard_map/all_gather | solution.py:60
  369.2 63.5 %gather_fusion.3 = bf16[16384,256]{1,0:T(8,128)(2,1)} fusion(bf16[8192,256]{1,0:T(8,128)(2,1)} %copy.20, s32[16384]{0:T(1024)S(1)} %broadcast_clamp_fusion.1), kind=kCustom, calls=%fused_computation.3 | custom fusion | bytes 16842752 | tf_op jit(solution)/shard_map/gather | solution.py:16
  432.8 8.1 %fusion.10 = f32[8,256,256,1]{1,2,3,0:T(8,128)S(1)} fusion(bf16[8,8,256,256]{3,2,1,0:T(8,128)(2,1)} %param.14, bf16[8,8,256,256]{3,2,1,0:T(8,128)(2,1)} %bitcast.60), kind=kOutput, calls=%fused_computation.34 | convolution fusion | flops 2147483648 | bytes 18874368 | tf_op jit(solution)/shard_map/bnij,bnjc->bic/dot_general | solution.py:17
  442.7 6.4 %copy.22 = bf16[8192,256]{1,0:T(8,128)(2,1)} copy(bf16[8192,256]{0,1:T(8,128)(2,1)} %all-gather.11.cloned.1.call-done) | data formatting | bytes 8388608 | tf_op jit(solution)/shard_map/all_gather | solution.py:24
  449.0 63.5 %gather_fusion.4 = bf16[16384,256]{1,0:T(8,128)(2,1)} fusion(bf16[8192,256]{1,0:T(8,128)(2,1)} %copy.22, s32[16384]{0:T(1024)S(1)} %broadcast_clamp_fusion), kind=kCustom, calls=%fused_computation.4 | custom fusion | bytes 16842752 | tf_op jit(solution)/shard_map/gather | solution.py:16
  512.6 8.1 %fusion.11 = f32[8,256,256,1]{1,2,3,0:T(8,128)S(1)} fusion(bf16[8,8,256,256]{3,2,1,0:T(8,128)(2,1)} %param.16, bf16[8,8,256,256]{3,2,1,0:T(8,128)(2,1)} %bitcast.61), kind=kOutput, calls=%fused_computation.35 | convolution fusion | flops 2147483648 | bytes 18874368 | tf_op jit(solution)/shard_map/bnij,bnjc->bic/dot_general | solution.py:17
  522.5 6.2 %add_divide_fusion = (f32[2048,128]{0,1:T(8,128)S(1)}, f32[2048,128]{0,1:T(8,128)}) fusion(f32[2048,128]{0,1:T(8,128)} %copy-done.5, f32[2048,128]{0,1:T(8,128)S(1)} %copy.39, f32[2048,128]{0,1:T(8,128)} %copy.38, f32[128]{0:T(128)S(1)} %copy-done.11, f32[2048]{0:T(1024)S(1)} %copy-done.10, f32[2048,128]{0,1:T(8,128)} %copy-done.6, f32[2048,128]{0,1:T(8,128)} %copy.37, ...), kind=kOutput, calls=%fused_computation.7 | convolution fusion | flops 541589504 | bytes 12853760 | tf_op jit(solution)/shard_map/dot_general | solution.py:39
  528.7 2.5 copy.24
  (74 shorter events, 18.0 us)
Async XLA Ops:
  7.2 58.2 %copy-start.1 = (f32[2048,128]{1,0:T(8,128)S(1)}, f32[2048,128]{1,0:T(8,128)}, u32[]{:S(2)}) copy-start(f32[2048,128]{1,0:T(8,128)} %param.10) | copy-start | bytes 3145732
  7.2 5.9 %copy-start.2 = (f32[2048,128]{1,0:T(8,128)S(1)}, f32[2048,128]{1,0:T(8,128)}, u32[]{:S(2)}) copy-start(f32[2048,128]{1,0:T(8,128)} %param.11) | copy-start | bytes 3145732
  7.2 60.4 %copy-start.7 = (s32[1,8192]{1,0:T(1,128)S(1)}, s32[1,8192]{1,0:T(1,128)}, u32[]{:S(2)}) copy-start(s32[1,8192]{1,0:T(1,128)} %param.18) | copy-start | bytes 98308
  7.2 61.2 %copy-start.8 = (s32[8,8]{1,0:T(8,128)S(1)}, s32[8,8]{1,0:T(8,128)}, u32[]{:S(2)}) copy-start(s32[8,8]{1,0:T(8,128)} %param.17) | copy-start | bytes 772
  7.2 62.0 %copy-start.9 = (s32[8,8]{1,0:T(8,128)S(1)}, s32[8,8]{1,0:T(8,128)}, u32[]{:S(2)}) copy-start(s32[8,8]{1,0:T(8,128)} %param.15) | copy-start | bytes 772
  7.2 62.2 %reduce-scatter.3.cloned.1.call-start = ((), (), s32[]{:S(2)}) async-start(), calls=%async_computation.4 | async-start | bytes 655360 | tf_op jit(solution)/shard_map/reduce_scatter | solution.py:29
  11.8 102.5 %all-gather.5.cloned.1.call-start = ((), (), s32[]{:S(2)}) async-start(), calls=%async_computation.2 | async-start | bytes 5242880 | tf_op jit(solution)/shard_map/all_gather | solution.py:60
  14.3 174.5 %all-gather.7.cloned.1.call-start = ((), (), s32[]{:S(2)}) async-start(), calls=%async_computation.3 | async-start | bytes 5242880 | tf_op jit(solution)/shard_map/all_gather | solution.py:24
  14.4 49.9 %collective-permute-start = (bf16[2048,256]{1,0:T(8,128)(2,1)}, bf16[2048,256]{1,0:T(8,128)(2,1)S(1)}, u32[]{:S(2)}, u32[]{:S(2)}) collective-permute-start(bf16[2048,256]{1,0:T(8,128)(2,1)} %pad_maximum_fusion), channel_id=1, source_target_pairs={{0,16},{4,20},{8,24},{12,28},{16,0},{20,4},{24,8},{28,12},{1,17},{... | collective-permute-start | bytes 3145736 | tf_op jit(solution)/shard_map/ppermute | solution.py:11
  64.3 1.0 copy-start.3
  65.3 254.8 %reduce-scatter.5.cloned.1.call-start = ((), (), s32[]{:S(2)}) async-start(), calls=%async_computation.7 | async-start | bytes 655360 | tf_op jit(solution)/shard_map/reduce_scatter | solution.py:29
  260.4 1.8 copy-start.10
  260.4 1.8 copy-start.11
  262.3 6.8 %copy-start = (bf16[2048,1024]{1,0:T(8,128)(2,1)S(1)}, bf16[2048,1024]{1,0:T(8,128)(2,1)}, u32[]{:S(2)}) copy-start(bf16[2048,1024]{1,0:T(8,128)(2,1)} %param.19) | copy-start | bytes 12582916
  267.7 1.0 copy-start.5
  267.8 1.3 copy-start.6
  270.6 92.2 %all-gather.9.cloned.1.call-start = ((), (), s32[]{:S(2)}) async-start(), calls=%async_computation.5 | async-start | bytes 5242880 | tf_op jit(solution)/shard_map/all_gather | solution.py:60
  271.8 170.9 %all-gather.11.cloned.1.call-start = ((), (), s32[]{:S(2)}) async-start(), calls=%async_computation.6 | async-start | bytes 5242880 | tf_op jit(solution)/shard_map/all_gather | solution.py:24
  271.8 47.3 %collective-permute-start.1 = (bf16[2048,256]{0,1:T(8,128)(2,1)}, bf16[2048,256]{0,1:T(8,128)(2,1)S(1)}, u32[]{:S(2)}, u32[]{:S(2)}) collective-permute-start(bf16[2048,256]{0,1:T(8,128)(2,1)} %pad_maximum_fusion.1), channel_id=1, source_target_pairs={{0,16},{4,20},{8,24},{12,28},{16,0},{20,4},{24,8},{28,12},{1,17},{... | collective-permute-start | bytes 3145736 | tf_op jit(solution)/shard_map/ppermute | solution.py:11
  319.1 1.0 copy-start.4
Sparse Core Ops, SparseCore 0:
  11.9 24.3 reduce-scatter.2
  38.5 34.4 all-gather.4
  74.7 34.4 all-gather.6
  270.8 18.9 reduce-scatter.4
  291.8 34.4 all-gather.8
  327.7 35.5 all-gather.10
where the time goes:
time: 540 us; the launch traced here: 539 us
  local copies, waits for them, and re-layouts  285 us (53%)
  waiting for transfers between devices  93.2 us (17%)
  blocking collectives  87.6 us (16%)
  matrix products  50.1 us (9%)
  between operations  14.5 us (3%)
    gather x4, local copies, waits for them, and re-layouts, block_product(): tiles = source[indices]  254 us
    ppermute x2, waiting for transfers between devices, swapped(): lax.ppermute(array, axis, [(i, i ^ 1 << stride) for i in range(lax.axis_s...  93 us
    psum x2, blocking collectives, exchange_term(): share = lax.psum(share, 'wide')  75.5 us
    dot_general x4, matrix products, block_product(): jnp.einsum('bnij,bnjc->bic', kernel, tiles, preferred_element_type=jnp.fl...  32.4 us
    unnamed x39, local copies, waits for them, and re-layouts  17.1 us
    all_gather x2, blocking collectives, exchange_term(): lax.all_gather(share.astype(jnp.bfloat16), 'narrow', axis=0, tiled=True)  12.1 us
    dot_general x2, matrix products, exchange_term(): jnp.dot(basis_cols, lax.all_gather(share.astype(jnp.bfloat16), 'narrow',...  11.7 us
  transfers between devices with their start and end apart: 8, of which 2 were waited for; matrix products, arithmetic and copies ran while one was open for 30% of the time, Pallas kernels for 0%

commit v1 on v0

v1 whole, which is shorter than its diff:
```python
import functools

import jax
import jax.numpy as jnp
from jax import lax
from jax.experimental import pallas as pl
from jax.experimental.pallas import tpu as pltpu
from jax.sharding import PartitionSpec as P

BLK = 256
APPS = 2
CH = 2
PIECES = 4
MESH = pl.DeviceIdType.MESH
F32 = jnp.float32
BF16 = jnp.bfloat16


def kernel(nw, nn, x_ref, y_ref, e_ref, s_ref, rl_ref, cl_ref, pr_ref, rk_ref, ck_ref, ub_ref,
           ox_ref, oy_ref,
           rkv, ckv, ubv, own0, own1, own2, own3, mir, stage, tile, perm, state, kres, wpart, wrs, wsnd, wrcv, wsum, wfull,
           ld_sem, z_s, z_r, py_s, py_r, ps_s, ps_r, pf_s, pf_r, my_s, my_r, ms_s, ms_r, mf_s, mf_r,
           rs_s, rs_r, wd_s, wd_r, ag_s, ag_r):
    owns = (own0, own1, own2, own3)
    w = lax.axis_index("wide")
    n = lax.axis_index("narrow")
    bits = nw.bit_length() - 1
    sib = n + 1 - 2 * lax.rem(n, 2)
    yp = lax.rem(n + 2, nn)
    ysib = lax.rem(sib + 2, nn)
    wpeers = [w + (1 << b) * (1 - 2 * lax.rem(w // (1 << b), 2)) for b in range(bits)]
    mirror = wpeers[bits - 1]

    rows = x_ref.shape[0]
    half = x_ref.shape[1] // 2
    blocks = rows // BLK
    nblk = rkv.shape[0] // blocks
    patch = rows * nn
    rank_share = ubv.shape[1] // nn

    loads = [
        pltpu.make_async_copy(ub_ref, ubv, ld_sem.at[0]),
        pltpu.make_async_copy(rk_ref, rkv, ld_sem.at[1]),
        pltpu.make_async_copy(ck_ref, ckv, ld_sem.at[2]),
    ]
    for load in loads:
        load.start()

    barrier = pltpu.get_barrier_semaphore()
    peers = [(w, lax.rem(n + j, nn)) for j in range(1, nn)] + [(p, n) for p in wpeers]
    for peer in peers:
        pl.semaphore_signal(barrier, inc=1, device_id=peer, device_id_type=MESH)

    low = lax.broadcasted_iota(jnp.int32, (BLK, 2 * half), 1) < half
    shift_row = jnp.broadcast_to(s_ref[...], (8, 2 * half))
    low8 = lax.broadcasted_iota(jnp.int32, (8, 2 * half), 1) < half
    turned = pltpu.roll(shift_row, half, 1)
    signed = [
        jnp.where(low8, -shift_row, turned)[0:1],
        jnp.where(low8, -turned, shift_row)[0:1],
    ]

    pending = []

    def send(src, dst, ssem, rsem, device):
        copy = pltpu.make_async_remote_copy(
            src_ref=src, dst_ref=dst, send_sem=ssem, recv_sem=rsem, device_id=device, device_id_type=MESH
        )
        copy.start()
        pending.append(copy)

    def arrived(ref, ssem, rsem, device):
        pltpu.make_async_remote_copy(
            src_ref=ref, dst_ref=ref, send_sem=ssem, recv_sem=rsem, device_id=device, device_id_type=MESH
        ).wait_recv()

    def part(buf, t, who, p):
        return buf.at[t, pl.ds(who * blocks + p * (blocks // PIECES), blocks // PIECES)]

    def held(t, who, p):
        return owns[t].at[pl.ds(who * blocks + p * (blocks // PIECES), blocks // PIECES)]

    def send_z(t, p):
        send(held(t, n, p), part(mir, t, n, p), z_s.at[t, p], z_r.at[t, p], (mirror, n))

    def send_own(t, p):
        send(held(t, n, p), held(t, n, p), py_s.at[t, p], py_r.at[t, p], (w, yp))
        send(held(t, n, p), held(t, n, p), ps_s.at[t, p], ps_r.at[t, p], (w, sib))

    def forward_own(t, p):
        arrived(held(t, yp, p), py_s.at[t, p], py_r.at[t, p], (w, yp))
        send(held(t, yp, p), held(t, yp, p), pf_s.at[t, p], pf_r.at[t, p], (w, sib))

    def finish_own(t):
        for p in range(PIECES):
            arrived(held(t, sib, p), ps_s.at[t, p], ps_r.at[t, p], (w, sib))
            arrived(held(t, ysib, p), pf_s.at[t, p], pf_r.at[t, p], (w, sib))

    def relay_z(t, p):
        arrived(part(mir, t, n, p), z_s.at[t, p], z_r.at[t, p], (mirror, n))
        send(part(mir, t, n, p), part(mir, t, n, p), my_s.at[t, p], my_r.at[t, p], (w, yp))
        send(part(mir, t, n, p), part(mir, t, n, p), ms_s.at[t, p], ms_r.at[t, p], (w, sib))

    def forward_mir(t, p):
        arrived(part(mir, t, yp, p), my_s.at[t, p], my_r.at[t, p], (w, yp))
        send(part(mir, t, yp, p), part(mir, t, yp, p), mf_s.at[t, p], mf_r.at[t, p], (w, sib))

    def finish_mir(t):
        for p in range(PIECES):
            arrived(part(mir, t, sib, p), ms_s.at[t, p], ms_r.at[t, p], (w, sib))
            arrived(part(mir, t, ysib, p), mf_s.at[t, p], mf_r.at[t, p], (w, sib))

    def project(t, c):
        z = state[c]
        summed = (z + pltpu.roll(z, half, 1)).astype(BF16)
        flipped = summed.T[:half]
        for q in range(nn):
            share = jnp.dot(flipped, ubv[:, q * rank_share:(q + 1) * rank_share], preferred_element_type=F32)
            wpart[t, q] = share.astype(BF16)

        for j in range(1, nn):
            to = lax.rem(n + j, nn)
            send(wpart.at[t, to], wrs.at[t, j - 1], rs_s.at[t, j - 1], rs_r.at[t, j - 1], (w, to))

    def wide_send(t, b):
        wsnd[t, b] = wsum[t].astype(BF16)
        send(wsnd.at[t, b], wrcv.at[t, b], wd_s.at[t, b], wd_r.at[t, b], (wpeers[b], n))

    def sum_narrow(t):
        total = wpart[t, n].astype(F32)
        for j in range(1, nn):
            arrived(wrs.at[t, j - 1], rs_s.at[t, j - 1], rs_r.at[t, j - 1], (w, lax.rem(n + j, nn)))
            total = total + wrs[t, j - 1].astype(F32)
        wsum[t] = total
        wide_send(t, 0)

    def sum_wide(t, b):
        arrived(wrcv.at[t, b], wd_s.at[t, b], wd_r.at[t, b], (wpeers[b], n))
        wsum[t] = wsum[t] + wrcv[t, b].astype(F32)
        if b + 1 < bits:
            wide_send(t, b + 1)
            return
        wfull[t, n] = wsum[t].astype(BF16)
        for j in range(1, nn):
            to = lax.rem(n + j, nn)
            send(wfull.at[t, n], wfull.at[t, n], ag_s.at[t, j - 1], ag_r.at[t, j - 1], (w, to))

    def finish_exchange(t):
        for j in range(1, nn):
            come = lax.rem(n - j + nn, nn)
            arrived(wfull.at[t, come], ag_s.at[t, j - 1], ag_r.at[t, j - 1], (w, lax.rem(n + j, nn)))

    def set_up(c):
        def body(i, _):
            at = pl.ds(pl.multiple_of(i * BLK, BLK), BLK)
            x, y = x_ref[at, :], y_ref[at, :]
            if c == 0:
                z = jnp.where(low, x, pltpu.roll(y, half, 1))
            else:
                z = jnp.where(low, pltpu.roll(x, half, 1), y)
            state[c, at, :] = z
            owns[c][n * blocks + i] = z.astype(BF16)
            return 0

        lax.fori_loop(0, blocks, body, 0)

    def block_sum(kernels, lists, source, b):
        total = jnp.zeros((BLK, 2 * half), F32)
        for k in range(nblk):
            total = total + jnp.dot(
                kernels[b * nblk + k], source[lists[b * nblk + k]], preferred_element_type=F32
            )
        return total

    def resonant(t, c):
        def body(b, _):
            kres[c, pl.ds(pl.multiple_of(b * BLK, BLK), BLK), :] = block_sum(
                rkv, rl_ref, owns[t], b
            )
            return 0

        lax.fori_loop(0, blocks, body, 0)

    def widen(t):
        def body(i, _):
            at = pl.ds(pl.multiple_of(i * BLK, BLK), BLK)
            stage[at, :] = mir[t, i].astype(F32)
            return 0

        lax.fori_loop(0, patch // BLK, body, 0)

    def permute(first, last):
        step = 64
        per = BLK // step

        def body(i, _):
            for g in range(per):
                base = i * BLK + g * step
                for j in range(step):
                    tile[j] = stage[pr_ref[base + j]]
                perm[i, g * step:(g + 1) * step, :] = tile[...].astype(BF16)
            return 0

        lax.fori_loop(first * patch // BLK // 4, last * patch // BLK // 4, body, 0)

    def update(a, c, first, last):
        t = a * CH + c
        sign = signed[c]

        def body(b, _):
            at = pl.ds(pl.multiple_of(b * BLK, BLK), BLK)
            kc = block_sum(ckv, cl_ref, perm, b)
            total = kres[c, at, :] + pltpu.roll(kc, half, 1)
            for q in range(nn):
                share = wfull[t, q]
                total = total + lax.dot_general(
                    ubv[at, q * rank_share:(q + 1) * rank_share],
                    jnp.concatenate([share, share], axis=0),
                    (((1,), (1,)), ((), ())),
                    preferred_element_type=F32,
                )
            level = e_ref[at, :]
            z = state[c, at, :]
            new = (level * z + total + sign * z) / (level + sign)
            if a + 1 < APPS:
                state[c, at, :] = new
                owns[t + CH][n * blocks + b] = new.astype(BF16)
            elif c == 0:
                state[c, at, :] = new
            else:
                z0 = state[0, at, :]
                ox_ref[at, :] = jnp.where(low, z0, pltpu.roll(new, half, 1))
                oy_ref[at, :] = jnp.where(low, pltpu.roll(z0, half, 1), new)
            return 0

        lax.fori_loop(first, last, body, 0)

    set_up(0)
    pl.semaphore_wait(barrier, len(peers))
    for p in range(PIECES):
        send_z(0, p)
        send_own(0, p)
    set_up(1)
    loads[0].wait()
    project(0, 0)
    project(1, 1)
    relay_z(0, 0)
    sum_narrow(0)
    sum_narrow(1)
    send_z(1, 0)
    for p in range(PIECES):
        forward_own(0, p)
        if p % 2 == 0:
            send_own(1, p)
    forward_mir(0, 0)
    for b in range(bits):
        sum_wide(0, b)
        sum_wide(1, b)
        if b == 0:
            relay_z(0, 1)
            send_z(1, 1)
    finish_own(0)
    loads[1].wait()
    resonant(0, 0)
    forward_mir(0, 1)
    relay_z(0, 2)
    send_z(1, 2)
    send_own(1, 1)
    send_own(1, 3)
    forward_mir(0, 2)
    relay_z(0, 3)
    send_z(1, 3)
    finish_exchange(0)
    finish_exchange(1)
    forward_mir(0, 3)
    loads[2].wait()

    quarter = blocks // 2
    total_t = APPS * CH
    for a in range(APPS):
        for c in range(CH):
            t = a * CH + c
            finish_mir(t)
            widen(t)
            later = t + 1 if t + 1 < total_t else None
            permute(0, 2)
            if later is not None:
                relay_z(later, 0)
            permute(2, 4)
            if later is not None:
                forward_mir(later, 0)
            update(a, c, 0, quarter)
            if a + 1 < APPS:
                for p in range(PIECES // 2):
                    send_z(t + CH, p)
            if later is not None:
                relay_z(later, 1)
            update(a, c, quarter, blocks)
            if a + 1 < APPS:
                for p in range(PIECES // 2, PIECES):
                    send_z(t + CH, p)
                for p in range(PIECES):
                    send_own(t + CH, p)
                project(t + CH, c)
            if later is None:
                continue
            forward_mir(later, 1)
            for p in range(PIECES):
                forward_own(later, p)
            finish_own(later)
            if a + 1 < APPS:
                sum_narrow(t + CH)
            resonant(later, later % CH)
            relay_z(later, 2)
            forward_mir(later, 2)
            if a + 1 < APPS:
                for b in range(bits):
                    sum_wide(t + CH, b)
            relay_z(later, 3)
            forward_mir(later, 3)
            if a + 1 < APPS:
                finish_exchange(t + CH)
    for copy in pending:
        copy.wait_send()


def on_device(nw, nn, trial_x, trial_y, energy, level_shift, resonant_kernel, resonant_list,
              coupling_kernel, coupling_list, partner, exchange_basis):
    rows, vectors = trial_x.shape
    rank = exchange_basis.shape[1]
    blocks, nblk = resonant_list.shape
    patch = rows * nn
    slots = APPS * CH
    bits = nw.bit_length() - 1
    half = vectors // 2
    share = rank // nn
    vmem = pl.BlockSpec(memory_space=pltpu.VMEM)
    smem = pl.BlockSpec(memory_space=pltpu.SMEM)
    anywhere = pl.BlockSpec(memory_space=pl.ANY)
    dma = pltpu.SemaphoreType.DMA
    pieces = [dma((slots, PIECES))] * 14
    flat = (blocks * nblk, BLK, BLK)
    new_x, new_y = pl.pallas_call(
        functools.partial(kernel, nw, nn),
        out_shape=[jax.ShapeDtypeStruct((rows, vectors), F32)] * 2,
        in_specs=[vmem] * 4 + [smem] * 3 + [anywhere] * 3,
        out_specs=[vmem] * 2,
        scratch_shapes=[
            pltpu.VMEM(flat, BF16),
            pltpu.VMEM(flat, BF16),
            pltpu.VMEM((rows, rank), BF16),
            *[pltpu.VMEM((patch // BLK, BLK, vectors), BF16)] * slots,
            pltpu.VMEM((slots, patch // BLK, BLK, vectors), BF16),
            pltpu.VMEM((patch, vectors), F32),
            pltpu.VMEM((64, vectors), F32),
            pltpu.VMEM((patch // BLK, BLK, vectors), BF16),
            pltpu.VMEM((CH, rows, vectors), F32),
            pltpu.VMEM((CH, rows, vectors), F32),
            pltpu.VMEM((slots, nn, half, share), BF16),
            pltpu.VMEM((slots, nn - 1, half, share), BF16),
            pltpu.VMEM((slots, bits, half, share), BF16),
            pltpu.VMEM((slots, bits, half, share), BF16),
            pltpu.VMEM((slots, half, share), F32),
            pltpu.VMEM((slots, nn, half, share), BF16),
            dma((3,)),
            *pieces,
            dma((slots, nn - 1)),
            dma((slots, nn - 1)),
            dma((slots, bits)),
            dma((slots, bits)),
            dma((slots, nn - 1)),
            dma((slots, nn - 1)),
        ],
        compiler_params=pltpu.CompilerParams(
            collective_id=0, has_side_effects=True, vmem_limit_bytes=63 * 1024 * 1024
        ),
    )(
        trial_x,
        trial_y,
        energy[:, None],
        level_shift[None, :],
        resonant_list.reshape(-1),
        coupling_list.reshape(-1),
        partner.reshape(-1),
        resonant_kernel.reshape(flat),
        coupling_kernel.reshape(flat),
        exchange_basis,
    )
    return new_x, new_y


def solution(mesh):
    nw, nn = mesh.shape["wide"], mesh.shape["narrow"]
    rows = P(("wide", "narrow"), None)
    return jax.shard_map(
        functools.partial(on_device, nw, nn),
        mesh=mesh,
        in_specs=(
            rows,
            rows,
            P(("wide", "narrow")),
            P(),
            P(("wide", "narrow"), None, None, None),
            rows,
            P(("wide", "narrow"), None, None, None),
            rows,
            P("wide", None),
            rows,
        ),
        out_specs=(rows, rows),
        check_vma=False,
    )
```

time: 540 us -> 218 us (0.40)
  local copies, waits for them, and re-layouts: 285 us -> 9.14 us
  Pallas kernels: 0 us -> 208 us
  waiting for transfers between devices: 93.2 us -> 0 us
  blocking collectives: 87.6 us -> 0 us
  matrix products: 50.1 us -> 0 us
  between operations: 14.5 us -> 0.64 us
    gather x5 -> x0, local copies, waits for them, and re-layouts: 255 us -> none  [the longest x4 254 us: block_product(): tiles = source[indices]]
    pallas_call x0 -> x1, Pallas kernels: none -> 208 us  [on_device(): pl.pallas_call(functools.partial(kernel, nw, nn), out_shape=[jax.ShapeDty...]
    ppermute x2 -> x0, waiting for transfers between devices: 93 us -> none  [swapped(): lax.ppermute(array, axis, [(i, i ^ 1 << stride) for i in range(lax.axis_s...]
    psum x2 -> x0, blocking collectives: 75.5 us -> none  [exchange_term(): share = lax.psum(share, 'wide')]
    dot_general x8 -> x0, matrix products: 50.1 us -> none  [the longest x4 32.4 us: block_product(): jnp.einsum('bnij,bnjc->bic', kernel, tiles, preferred_element_type=jnp.fl...]
    all_gather x2 -> x0, local copies, waits for them, and re-layouts: 12.7 us -> none  [the longest x1 6.37 us: mirror_rows(): return lax.all_gather(moved, 'narrow', axis=0, tiled=True)]
    unnamed x39 -> x2, local copies, waits for them, and re-layouts: 17.1 us -> 4.52 us
    all_gather x2 -> x0, blocking collectives: 12.1 us -> none  [exchange_term(): lax.all_gather(share.astype(jnp.bfloat16), 'narrow', axis=0, tiled=True)]
  transfers between devices with their start and end apart: 8 -> 0, of which waited for: 2 -> 0; matrix products, arithmetic and copies ran while one was open for 30% -> 0% of each run, Pallas kernels for 0% -> 0%
where the time goes in v1:
time: 218 us; the launch traced here: 217 us
  Pallas kernels  208 us (95%)
  local copies, waits for them, and re-layouts  9.14 us (4%)
    pallas_call x1, Pallas kernels, on_device(): pl.pallas_call(functools.partial(kernel, nw, nn), out_shape=[jax.ShapeDty...  208 us
    unnamed x2, local copies, waits for them, and re-layouts  4.52 us

profile of v1, /device:TPU:0, one launch (start us, length us, event | category | flops | bytes accessed | tf_op | source)
XLA Modules:
  0.0 217.4 jit_solution(9285096072638937476)
XLA Ops:
  0.6 1.3 reshape.19.rl_ref
  1.9 1.3 reshape.20.cl_ref
  3.2 2.0 copy.12.e_ref
  5.3 207.6 %shard_map.113 = (f32[2048,128]{1,0:T(8,128)}, f32[2048,128]{1,0:T(8,128)}) custom-call(f32[2048,128]{1,0:T(8,128)} %x_ref.1, f32[2048,128]{1,0:T(8,128)} %y_ref.1, f32[2048,1]{1,0:T(8,128)} %copy.12.e_ref, f32[1,128]{1,0:T(1,128)} %bitcast.9, s32[64]{0:T(128)} %reshape.19.rl_ref, s32[64]{0:T(128)} %reshape.20.cl_ref, s32[8192]{0:T(1024)} %bitcast.7, ...), custom_call_target="tpu_custom_call" | custom-call | tf_op jit(solution)/shard_map/pallas_call | solution.py:343
  212.9 2.3 %copy.15 = f32[2048,128]{1,0:T(8,128)} copy(f32[2048,128]{1,0:T(8,128)} %get-tuple-element.4) | data formatting | bytes 2097152
  215.2 2.3 %copy.16 = f32[2048,128]{1,0:T(8,128)} copy(f32[2048,128]{1,0:T(8,128)} %get-tuple-element.5) | data formatting | bytes 2097152

commit v2 on v1

--- a/solution.py
+++ b/solution.py
@@ -30,6 +30,7 @@
     ysib = lax.rem(sib + 2, nn)
     wpeers = [w + (1 << b) * (1 - 2 * lax.rem(w // (1 << b), 2)) for b in range(bits)]
     mirror = wpeers[bits - 1]
+    wpeers = wpeers[::-1]
 
     rows = x_ref.shape[0]
     half = x_ref.shape[1] // 2
@@ -116,27 +117,27 @@
         flipped = summed.T[:half]
         for q in range(nn):
             share = jnp.dot(flipped, ubv[:, q * rank_share:(q + 1) * rank_share], preferred_element_type=F32)
-            wpart[t, q] = share.astype(BF16)
+            wpart[t, q] = share
 
         for j in range(1, nn):
             to = lax.rem(n + j, nn)
             send(wpart.at[t, to], wrs.at[t, j - 1], rs_s.at[t, j - 1], rs_r.at[t, j - 1], (w, to))
 
     def wide_send(t, b):
-        wsnd[t, b] = wsum[t].astype(BF16)
+        wsnd[t, b] = wsum[t]
         send(wsnd.at[t, b], wrcv.at[t, b], wd_s.at[t, b], wd_r.at[t, b], (wpeers[b], n))
 
     def sum_narrow(t):
-        total = wpart[t, n].astype(F32)
+        total = wpart[t, n]
         for j in range(1, nn):
             arrived(wrs.at[t, j - 1], rs_s.at[t, j - 1], rs_r.at[t, j - 1], (w, lax.rem(n + j, nn)))
-            total = total + wrs[t, j - 1].astype(F32)
+            total = total + wrs[t, j - 1]
         wsum[t] = total
         wide_send(t, 0)
 
     def sum_wide(t, b):
         arrived(wrcv.at[t, b], wd_s.at[t, b], wd_r.at[t, b], (wpeers[b], n))
-        wsum[t] = wsum[t] + wrcv[t, b].astype(F32)
+        wsum[t] = wsum[t] + wrcv[t, b]
         if b + 1 < bits:
             wide_send(t, b + 1)
             return
@@ -237,70 +238,83 @@
 
     set_up(0)
     pl.semaphore_wait(barrier, len(peers))
-    for p in range(PIECES):
-        send_z(0, p)
-        send_own(0, p)
+    send_z(0, 0)
+    send_z(0, 1)
+    send_own(0, 0)
     set_up(1)
     loads[0].wait()
     project(0, 0)
     project(1, 1)
+    for p in range(1, PIECES):
+        send_own(0, p)
     relay_z(0, 0)
+    send_z(0, 2)
     sum_narrow(0)
     sum_narrow(1)
+    send_z(0, 3)
+    forward_own(0, 0)
+    forward_mir(0, 0)
+    relay_z(0, 1)
     send_z(1, 0)
-    for p in range(PIECES):
+    for p in range(1, PIECES):
         forward_own(0, p)
-        if p % 2 == 0:
-            send_own(1, p)
-    forward_mir(0, 0)
-    for b in range(bits):
-        sum_wide(0, b)
-        sum_wide(1, b)
-        if b == 0:
-            relay_z(0, 1)
-            send_z(1, 1)
     finish_own(0)
     loads[1].wait()
     resonant(0, 0)
+    relay_z(0, 2)
+    send_z(1, 1)
+    send_own(1, 0)
     forward_mir(0, 1)
-    relay_z(0, 2)
+    sum_wide(0, 0)
+    sum_wide(1, 0)
+    forward_mir(0, 2)
+    send_own(1, 1)
+    relay_z(0, 3)
     send_z(1, 2)
-    send_own(1, 1)
+    for b in range(1, bits - 1):
+        sum_wide(0, b)
+        sum_wide(1, b)
+    forward_mir(0, 3)
+    send_z(1, 3)
+    send_own(1, 2)
     send_own(1, 3)
-    forward_mir(0, 2)
-    relay_z(0, 3)
-    send_z(1, 3)
-    finish_exchange(0)
-    finish_exchange(1)
-    forward_mir(0, 3)
+    sum_wide(0, bits - 1)
+    sum_wide(1, bits - 1)
     loads[2].wait()
 
-    quarter = blocks // 2
+    middle = blocks // 2
     total_t = APPS * CH
     for a in range(APPS):
         for c in range(CH):
             t = a * CH + c
+            later = t + 1 if t + 1 < total_t else None
+            more = a + 1 < APPS
             finish_mir(t)
             widen(t)
-            later = t + 1 if t + 1 < total_t else None
-            permute(0, 2)
+            permute(0, 1)
+            if a > 0:
+                for b in range(1, bits - 1):
+                    sum_wide(t, b)
+            permute(1, 2)
             if later is not None:
                 relay_z(later, 0)
-            permute(2, 4)
+            permute(2, 3)
+            if a > 0:
+                sum_wide(t, bits - 1)
+            permute(3, 4)
             if later is not None:
                 forward_mir(later, 0)
-            update(a, c, 0, quarter)
-            if a + 1 < APPS:
+            finish_exchange(t)
+            update(a, c, 0, middle)
+            if more:
                 for p in range(PIECES // 2):
                     send_z(t + CH, p)
             if later is not None:
                 relay_z(later, 1)
-            update(a, c, quarter, blocks)
-            if a + 1 < APPS:
+            update(a, c, middle, blocks)
+            if more:
                 for p in range(PIECES // 2, PIECES):
                     send_z(t + CH, p)
-                for p in range(PIECES):
-                    send_own(t + CH, p)
                 project(t + CH, c)
             if later is None:
                 continue
@@ -308,18 +322,18 @@
             for p in range(PIECES):
                 forward_own(later, p)
             finish_own(later)
-            if a + 1 < APPS:
-                sum_narrow(t + CH)
             resonant(later, later % CH)
             relay_z(later, 2)
             forward_mir(later, 2)
-            if a + 1 < APPS:
-                for b in range(bits):
-                    sum_wide(t + CH, b)
+            if more:
+                sum_narrow(t + CH)
             relay_z(later, 3)
+            if more:
+                for p in range(PIECES):
+                    send_own(t + CH, p)
             forward_mir(later, 3)
-            if a + 1 < APPS:
-                finish_exchange(t + CH)
+            if later // CH > 0:
+                sum_wide(later, 0)
     for copy in pending:
         copy.wait_send()
 
@@ -356,10 +370,10 @@
             pltpu.VMEM((patch // BLK, BLK, vectors), BF16),
             pltpu.VMEM((CH, rows, vectors), F32),
             pltpu.VMEM((CH, rows, vectors), F32),
-            pltpu.VMEM((slots, nn, half, share), BF16),
-            pltpu.VMEM((slots, nn - 1, half, share), BF16),
-            pltpu.VMEM((slots, bits, half, share), BF16),
-            pltpu.VMEM((slots, bits, half, share), BF16),
+            pltpu.VMEM((slots, nn, half, share), F32),
+            pltpu.VMEM((slots, nn - 1, half, share), F32),
+            pltpu.VMEM((slots, bits, half, share), F32),
+            pltpu.VMEM((slots, bits, half, share), F32),
             pltpu.VMEM((slots, half, share), F32),
             pltpu.VMEM((slots, nn, half, share), BF16),
             dma((3,)),

time: 218 us -> 184 us (0.84)
  Pallas kernels: 208 us -> 174 us
    pallas_call x1, Pallas kernels: 208 us -> 174 us  [on_device(): pl.pallas_call(functools.partial(kernel, nw, nn), out_shape=[jax.ShapeDty...]
where the time goes in v2:
time: 184 us
  Pallas kernels  174 us (95%)
  local copies, waits for them, and re-layouts  9.14 us (5%)
    pallas_call x1, Pallas kernels, on_device(): pl.pallas_call(functools.partial(kernel, nw, nn), out_shape=[jax.ShapeDty...  174 us
    unnamed x2, local copies, waits for them, and re-layouts  4.52 us

profile of v2, /device:TPU:0, one launch (start us, length us, event | category | flops | bytes accessed | tf_op | source)
XLA Modules:
  0.0 183.8 jit_solution(6120598745178376627)
XLA Ops:
  0.6 1.3 reshape.19.rl_ref
  1.9 1.3 reshape.20.cl_ref
  3.2 2.0 %copy.12.e_ref = f32[2048,1]{1,0:T(8,128)} copy(f32[2048,1]{0,1:T(1,128)} %bitcast.8) | data formatting | bytes 16384 | tf_op jit(solution)/shard_map/broadcast_in_dim | solution.py:394
  5.3 174.0 %shard_map.113 = (f32[2048,128]{1,0:T(8,128)}, f32[2048,128]{1,0:T(8,128)}) custom-call(f32[2048,128]{1,0:T(8,128)} %x_ref.1, f32[2048,128]{1,0:T(8,128)} %y_ref.1, f32[2048,1]{1,0:T(8,128)} %copy.12.e_ref, f32[1,128]{1,0:T(1,128)} %bitcast.9, s32[64]{0:T(128)} %reshape.19.rl_ref, s32[64]{0:T(128)} %reshape.20.cl_ref, s32[8192]{0:T(1024)} %bitcast.7, ...), custom_call_target="tpu_custom_call" | custom-call | tf_op jit(solution)/shard_map/pallas_call | solution.py:357
  179.3 2.3 %copy.15 = f32[2048,128]{1,0:T(8,128)} copy(f32[2048,128]{1,0:T(8,128)} %get-tuple-element.4) | data formatting | bytes 2097152
  181.5 2.3 %copy.16 = f32[2048,128]{1,0:T(8,128)} copy(f32[2048,128]{1,0:T(8,128)} %get-tuple-element.5) | data formatting | bytes 2097152
